TPU v7x, 256 devices: a whole 4x4x8 slice. The times are simulated.
256 devices in a mesh: rows: 4 (over y_lo, core), shard: 64 (over x, y_hi, z).
Axes of the slice: x: 4, y: 4 (y_hi: 2, y_lo: 2; y = y_hi * 2 + y_lo), z: 8, core: 2. Of those that a mesh axis runs over, the one named last changes fastest.
Arguments:
- hidden_in: bfloat16 [128, 14336], P('rows', 'shard'), may hold values from -6 to 6
- resid: bfloat16 [128, 3584], P('rows'), may hold values from -6 to 6
- down_one: bfloat16 [14336, 3584], P('shard'), may hold values from -0.046875 to 0.046875
- gain_one: float32 [3584], replicated, may hold values from 0.5 to 1.5
- enc_weight: bfloat16 [3584, 65536], P(None, ('rows', 'shard')), may hold values from -0.09375 to 0.09375
- enc_bias: float32 [65536], P(('rows', 'shard')), may hold values from -3 to 3
- dec_weight: bfloat16 [65536, 3584], P(('rows', 'shard')), may hold values from -0.09375 to 0.09375
- dec_bias: float32 [3584], replicated, may hold values from -3 to 3
- gain_pre: float32 [3584], replicated, may hold values from 0.5 to 1.5
- gate_two: bfloat16 [3584, 14336], P(None, 'shard'), may hold values from -0.09375 to 0.09375
- up_two: bfloat16 [3584, 14336], P(None, 'shard'), may hold values from -0.09375 to 0.09375
- down_two: bfloat16 [14336, 3584], P('shard'), may hold values from -0.046875 to 0.046875
- gain_post: float32 [3584], replicated, may hold values from 0.5 to 1.5
Outputs:
- latents: bfloat16 [128, 65536], P(None, ('rows', 'shard'))
- delta: float32 [128, 3584], P('rows', 'shard')
All inputs are finite; a program needn't handle non-finite values.
Results may differ from a plain program's by a relative error of at most 0.0064.
Values may be sent and summed in bfloat16 or wider, within the bound.
A program may use at most 64 MiB of HBM per device.

v0:
```python
import jax
import jax.numpy as jnp
from jax import lax
from jax.sharding import PartitionSpec as P

D = 3584


def on_device(
    hidden_in,
    resid,
    down_one,
    gain_one,
    enc_weight,
    enc_bias,
    dec_weight,
    dec_bias,
    gain_pre,
    gate_two,
    up_two,
    down_two,
    gain_post,
):
    n_shard = lax.axis_size("shard")
    columns = D // n_shard
    offset = lax.axis_index("shard") * columns
    first_part = jnp.dot(hidden_in, down_one, preferred_element_type=jnp.float32)
    first = lax.psum(first_part, "shard")
    mean_sq = jnp.mean(first * first, axis=1, keepdims=True)
    clean = (resid.astype(jnp.float32) + first * lax.rsqrt(mean_sq + 1e-06) * gain_one).astype(
        jnp.bfloat16
    )
    clean_all = lax.all_gather(clean, "rows", axis=0, tiled=True)
    centered = (clean_all.astype(jnp.float32) - dec_bias).astype(jnp.bfloat16)
    pre_act = jnp.dot(centered, enc_weight, preferred_element_type=jnp.float32) + enc_bias
    latents = jnp.maximum(pre_act, 0.0).astype(jnp.bfloat16)
    group_sums = lax.psum_scatter(
        jnp.dot(latents, dec_weight, preferred_element_type=jnp.float32),
        "rows",
        scatter_dimension=0,
        tiled=True,
    )
    total = lax.psum(group_sums, "shard")
    recon = (total + dec_bias).astype(jnp.bfloat16)
    stream = jnp.concatenate([clean, recon], axis=0)
    upcast = stream.astype(jnp.float32)
    in_sq = jnp.mean(upcast * upcast, axis=1, keepdims=True)
    normed = (upcast * lax.rsqrt(in_sq + 1e-06) * gain_pre).astype(jnp.bfloat16)
    gate_out = jnp.dot(normed, gate_two, preferred_element_type=jnp.float32)
    up_out = jnp.dot(normed, up_two, preferred_element_type=jnp.float32)
    act = (jax.nn.gelu(gate_out, approximate=True) * up_out).astype(jnp.bfloat16)
    second_part = jnp.dot(act, down_two, preferred_element_type=jnp.float32)
    second_cols = lax.psum_scatter(second_part, "shard", scatter_dimension=1, tiled=True)
    second_sq = lax.psum(jnp.sum(second_cols * second_cols, axis=1), "shard")
    stream_cols = lax.dynamic_slice_in_dim(upcast, offset, columns, 1)
    post_cols = lax.dynamic_slice_in_dim(gain_post, offset, columns, 0)
    outputs = stream_cols + second_cols * lax.rsqrt(second_sq[:, None] / D + 1e-06) * post_cols
    half = clean.shape[0]
    delta = outputs[half:] - outputs[:half]
    return (latents, delta)


def solution(mesh):
    in_specs = (
        P("rows", "shard"),
        P("rows", None),
        P("shard", None),
        P(),
        P(None, ("rows", "shard")),
        P(("rows", "shard")),
        P(("rows", "shard"), None),
        P(),
        P(),
        P(None, "shard"),
        P(None, "shard"),
        P("shard", None),
        P(),
    )
    out_specs = (P(None, ("rows", "shard")), P("rows", "shard"))
    return jax.shard_map(
        on_device, mesh=mesh, in_specs=in_specs, out_specs=out_specs, check_vma=False
    )
```

profile of v0, /device:TPU:8, one launch (start us, length us, event | category | flops | bytes accessed | tf_op | source)
XLA Modules:
  0.0 2275.2 jit_solution(13110349626699264122)
XLA Ops:
  7.2 0.0 all-reduce.5.cloned.1.call-start
  7.2 2.7 fusion.22
  10.0 0.0 reduce-scatter.3.cloned.1.call-start
  10.1 678.9 %all-reduce.5.cloned.1.call-done = f32[32,3584]{1,0:T(8,128)} async-done(((f32[32,3584]{1,0:T(8,128)}), f32[32,3584]{1,0:T(8,128)}) %all-reduce.5.cloned.1.call-update) | async-done | bytes 458768 | tf_op jit(solution)/shard_map/psum | solution.py:28
  689.0 1.3 multiply_reduce_fusion.1
  690.3 1.2 add_convert_fusion.1
  691.5 8.9 all_gather.3
  700.4 0.4 fusion.1
  700.9 1.7 fusion.23
  702.6 0.0 all-reduce.7.cloned.1.call-start
  702.6 22.3 reduce-scatter.3.cloned.1.call-done
  725.0 680.6 %all-reduce.7.cloned.1.call-done = f32[32,3584]{1,0:T(8,128)} async-done(((f32[32,3584]{1,0:T(8,128)}), f32[32,3584]{1,0:T(8,128)}) %all-reduce.7.cloned.1.call-update) | async-done | bytes 458768 | tf_op jit(solution)/shard_map/psum | solution.py:43
  1405.6 1.0 add_convert_fusion
  1406.7 0.2 multiply_reduce_fusion
  1406.9 2.1 fusion.21
  1409.0 4.3 fusion.3
  1413.3 0.6 dynamic-slice
  1414.5 0.8 dynamic_slice.7
  1415.3 0.1 maximum_convert_fusion
  1415.3 672.4 %all-reduce.9.cloned.1.call-done = f32[64,3584]{1,0:T(8,128)} async-done(((f32[64,3584]{1,0:T(8,128)}), f32[64,3584]{1,0:T(8,128)}) %all-reduce.9.cloned.1.call-update) | async-done | bytes 917520
  2087.8 1.0 multiply_reduce_fusion.2
  2088.8 178.3 %psum.23 = f32[64]{0:T(128)S(1)} all-reduce(f32[64]{0:T(128)S(1)} %multiply_reduce_fusion.2), channel_id=1, replica_groups=mesh['rows'=4,'shard'=64] {'shard'}, use_global_device_ids=true, to_apply=%region_7.0 | all-reduce | flops 64 | bytes 512 | tf_op jit(solution)/shard_map/psum | solution.py:54
  2267.1 0.9 multiply_add_fusion
  2268.0 0.6 slice_subtract_fusion
  (26 shorter events, 0.2 us)
Async XLA Ops:
  7.2 693.7 %copy-start = (bf16[256,3584]{1,0:T(8,128)(2,1)S(1)}, bf16[256,3584]{1,0:T(8,128)(2,1)}, u32[]{:S(2)}) copy-start(bf16[256,3584]{1,0:T(8,128)(2,1)} %param.19) | copy-start | bytes 5505028
  7.2 683.1 %copy-start.1 = (bf16[32,3584]{1,0:T(8,128)(2,1)S(1)}, bf16[32,3584]{1,0:T(8,128)(2,1)}, u32[]{:S(2)}) copy-start(bf16[32,3584]{1,0:T(8,128)(2,1)} %param.14) | copy-start | bytes 688132
  7.2 683.1 %copy-start.3 = (f32[3584]{0:T(1024)S(1)}, f32[3584]{0:T(1024)}, u32[]{:S(2)}) copy-start(f32[3584]{0:T(1024)} %param.16) | copy-start | bytes 43012
  7.2 681.8 %all-reduce.5.cloned.1.call-start = ((), (), s32[]{:S(2)}) async-start(), calls=%async_computation.1 | async-start | bytes 917504 | tf_op jit(solution)/shard_map/psum | solution.py:28
  10.0 690.4 %copy-start.5 = (f32[3584]{0:T(1024)S(1)}, f32[3584]{0:T(1024)}, u32[]{:S(2)}) copy-start(f32[3584]{0:T(1024)} %param.20) | copy-start | bytes 43012
  10.0 690.4 %copy-start.7 = (f32[256]{0:T(256)S(1)}, f32[256]{0:T(256)}, u32[]{:S(2)}) copy-start(f32[256]{0:T(256)} %param.18) | copy-start | bytes 3076
  10.0 714.9 %reduce-scatter.3.cloned.1.call-start = ((), (), s32[]{:S(2)}) async-start(), calls=%async_computation.2 | async-start | bytes 2293760 | tf_op jit(solution)/shard_map/reduce_scatter | solution.py:37
  689.0 11.4 copy-start.6
  700.8 1.7 copy-start.2
  702.5 704.4 %copy-start.4 = (f32[3584]{0:T(1024)S(1)}, f32[3584]{0:T(1024)}, u32[]{:S(2)}) copy-start(f32[3584]{0:T(1024)} %param.21) | copy-start | bytes 43012
  702.6 703.1 %all-reduce.7.cloned.1.call-start = ((), (), s32[]{:S(2)}) async-start(), calls=%async_computation.3 | async-start | bytes 917504 | tf_op jit(solution)/shard_map/psum | solution.py:43
  725.0 1362.8 %all-reduce.9.cloned.1.call-start = ((), (), s32[]{:S(2)}) async-start(), calls=%async_computation.4 | async-start | bytes 1835008
  1408.9 4.3 copy-start.8
Sparse Core Ops, SparseCore 0:
  10.7 678.3 all-reduce.4
  702.7 22.2 reduce-scatter.2
  727.7 677.8 all-reduce.6
  1413.4 674.3 all-reduce.8
where the time goes:
time: 2280 us
  waiting for transfers between devices  2050 us (90%)
  blocking collectives  187 us (8%)
    psum x1, waiting for transfers between devices, on_device(): total = lax.psum(group_sums, 'shard')  681 us
    psum x1, waiting for transfers between devices, on_device(): first = lax.psum(first_part, 'shard')  679 us
    unnamed x5, waiting for transfers between devices  673 us
    psum x1, blocking collectives, on_device(): second_sq = lax.psum(jnp.sum(second_cols * second_cols, axis=1), 'shard')  178 us
  transfers between devices with their start and end apart: 4, of which 4 were waited for; matrix products, arithmetic and copies ran while one was open for 0% of the time, Pallas kernels for 0%

commit v1 on v0

--- a/solution.py
+++ b/solution.py
@@ -40,7 +40,7 @@
         scatter_dimension=0,
         tiled=True,
     )
-    total = lax.psum(group_sums, "shard")
+    total = jnp.sum(lax.all_gather(group_sums, "shard"), axis=0)
     recon = (total + dec_bias).astype(jnp.bfloat16)
     stream = jnp.concatenate([clean, recon], axis=0)
     upcast = stream.astype(jnp.float32)

time: 2280 us -> 1900 us (0.83)
  waiting for transfers between devices: 2050 us -> 1670 us
    psum x1 -> x0, waiting for transfers between devices: 681 us -> none  [on_device(): total = lax.psum(group_sums, 'shard')]
    all_gather x0 -> x1, waiting for transfers between devices: none -> 296 us  [on_device(): total = jnp.sum(lax.all_gather(group_sums, 'shard'), axis=0)]
where the time goes in v1:
time: 1900 us
  waiting for transfers between devices  1670 us (88%)
  blocking collectives  187 us (10%)
    psum x1, waiting for transfers between devices, on_device(): first = lax.psum(first_part, 'shard')  679 us
    unnamed x5, waiting for transfers between devices  675 us
    all_gather x1, waiting for transfers between devices, on_device(): total = jnp.sum(lax.all_gather(group_sums, 'shard'), axis=0)  296 us
    psum x1, blocking collectives, on_device(): second_sq = lax.psum(jnp.sum(second_cols * second_cols, axis=1), 'shard')  178 us
  transfers between devices with their start and end apart: 4, of which 4 were waited for; matrix products, arithmetic and copies ran while one was open for 0% of the time, Pallas kernels for 0%

profile of v1, /device:TPU:8, one launch (start us, length us, event | category | flops | bytes accessed | tf_op | source)
XLA Modules:
  0.0 1903.1 jit_solution(3859037385104535289)
XLA Ops:
  7.2 2.7 fusion.22
  10.0 0.0 reduce-scatter.3.cloned.1.call-start
  10.1 678.9 %all-reduce.4.cloned.1.call-done = f32[32,3584]{1,0:T(8,128)} async-done(((f32[32,3584]{1,0:T(8,128)}), f32[32,3584]{1,0:T(8,128)}) %all-reduce.4.cloned.1.call-update) | async-done | bytes 458768 | tf_op jit(solution)/shard_map/psum | solution.py:28
  689.0 1.3 multiply_reduce_fusion.1
  690.3 1.2 add_convert_fusion.1
  691.5 8.9 all_gather.9
  700.4 0.4 fusion.1
  700.9 1.7 fusion.23
  702.6 0.0 all-gather.3.cloned.1.call-start
  702.6 22.3 %reduce-scatter.3.cloned.1.call-done = f32[32,3584]{1,0:T(8,128)} async-done(((f32[128,3584]{1,0:T(8,128)}), f32[32,3584]{1,0:T(8,128)}) %reduce-scatter.3.cloned.1.call-update) | async-done | bytes 458768 | tf_op jit(solution)/shard_map/reduce_scatter | solution.py:37
  725.0 0.0 all-reduce.6.cloned.1.call-start
  725.0 296.4 %all-gather.3.cloned.1.call-done = f32[2048,3584]{1,0:T(8,128)} async-done(((f32[32,3584]{1,0:T(8,128)}), f32[2048,3584]{1,0:T(8,128)}) %all-gather.3.cloned.1.call-update) | async-done | bytes 29360144 | tf_op jit(solution)/shard_map/all_gather | solution.py:43
  1021.4 10.7 reduce_sum.37
  1032.2 0.2 multiply_reduce_fusion
  1032.4 2.1 fusion.21
  1034.4 4.3 fusion.3
  1038.7 0.6 dynamic-slice
  1040.0 0.8 dynamic_slice.7
  1040.8 0.1 maximum_convert_fusion
  1040.8 674.9 %all-reduce.6.cloned.1.call-done = f32[64,3584]{1,0:T(8,128)} async-done(((f32[64,3584]{1,0:T(8,128)}), f32[64,3584]{1,0:T(8,128)}) %all-reduce.6.cloned.1.call-update) | async-done | bytes 917520
  1715.7 1.0 multiply_reduce_fusion.2
  1716.8 178.3 %psum.15 = f32[64]{0:T(128)S(1)} all-reduce(f32[64]{0:T(128)S(1)} %multiply_reduce_fusion.2), channel_id=1, replica_groups=mesh['rows'=4,'shard'=64] {'shard'}, use_global_device_ids=true, to_apply=%region_7.0 | all-reduce | flops 64 | bytes 512 | tf_op jit(solution)/shard_map/psum | solution.py:54
  1895.1 0.9 multiply_add_fusion
  1896.0 0.6 slice_subtract_fusion
  (27 shorter events, 0.2 us)
Async XLA Ops:
  7.2 693.7 %copy-start = (bf16[256,3584]{1,0:T(8,128)(2,1)S(1)}, bf16[256,3584]{1,0:T(8,128)(2,1)}, u32[]{:S(2)}) copy-start(bf16[256,3584]{1,0:T(8,128)(2,1)} %param.19) | copy-start | bytes 5505028
  7.2 683.1 %copy-start.1 = (bf16[32,3584]{1,0:T(8,128)(2,1)S(1)}, bf16[32,3584]{1,0:T(8,128)(2,1)}, u32[]{:S(2)}) copy-start(bf16[32,3584]{1,0:T(8,128)(2,1)} %param.14) | copy-start | bytes 688132
  7.2 683.1 %copy-start.3 = (f32[3584]{0:T(1024)S(1)}, f32[3584]{0:T(1024)}, u32[]{:S(2)}) copy-start(f32[3584]{0:T(1024)} %param.16) | copy-start | bytes 43012
  7.2 681.8 %all-reduce.4.cloned.1.call-start = ((), (), s32[]{:S(2)}) async-start(), calls=%async_computation.1 | async-start | bytes 917504 | tf_op jit(solution)/shard_map/psum | solution.py:28
  10.0 690.4 %copy-start.5 = (f32[3584]{0:T(1024)S(1)}, f32[3584]{0:T(1024)}, u32[]{:S(2)}) copy-start(f32[3584]{0:T(1024)} %param.20) | copy-start | bytes 43012
  10.0 690.4 %copy-start.7 = (f32[256]{0:T(256)S(1)}, f32[256]{0:T(256)}, u32[]{:S(2)}) copy-start(f32[256]{0:T(256)} %param.18) | copy-start | bytes 3076
  10.0 714.9 %reduce-scatter.3.cloned.1.call-start = ((), (), s32[]{:S(2)}) async-start(), calls=%async_computation.2 | async-start | bytes 2293760 | tf_op jit(solution)/shard_map/reduce_scatter | solution.py:37
  689.0 11.4 copy-start.6
  700.8 1.7 copy-start.2
  702.6 318.8 %all-gather.3.cloned.1.call-start = ((), (), s32[]{:S(2)}) async-start(), calls=%async_computation.3 | async-start | bytes 29818880 | tf_op jit(solution)/shard_map/all_gather | solution.py:43
  725.0 990.8 %all-reduce.6.cloned.1.call-start = ((), (), s32[]{:S(2)}) async-start(), calls=%async_computation.4 | async-start | bytes 1835008
  1021.4 11.0 copy-start.4
  1034.4 4.3 copy-start.8
Sparse Core Ops, SparseCore 0:
  10.7 678.3 all-reduce.3
  702.7 22.2 reduce-scatter.2
  729.2 292.1 all-gather.2
  1038.8 676.8 all-reduce.5
